TPU v7x, 32 devices: a whole 2x2x4 slice. The times are simulated.
32 devices in a mesh: groups: 2 (over y), dp: 4 (over z), tensor: 4 (over x, core).
Axes of the slice: x: 2, y: 2, z: 4, core: 2. Of those that a mesh axis runs over, the one named last changes fastest.
Arguments:
- output_gradient: bfloat16 [1024, 15872], P(('groups', 'dp'), 'tensor'), parts along dimension 0, may hold values from -6 to 6
- saved_layer_input: bfloat16 [1024, 14848], P(('groups', 'dp'), 'tensor'), parts along dimension 0, may hold values from -6 to 6
- adapter_middle: bfloat16 [1024, 64], P(('groups', 'dp')), parts along dimension 0, may hold values from -6 to 6
- frozen_weight: bfloat16 [14848, 15872], P('dp', 'tensor'), may hold values from -0.046875 to 0.046875
- block_row_scale: float32 [232, 15872], P('dp', 'tensor'), may hold values from 0.25 to 4
- adapter_down_weight: bfloat16 [8, 64, 14848], P('groups', None, 'dp'), parts along dimension 0, may hold values from -0.375 to 0.375
- adapter_up_weight: bfloat16 [8, 64, 15872], P('groups', None, 'tensor'), parts along dimension 0, may hold values from -0.046875 to 0.046875
- document_lengths: int32 [8, 4], P('groups'), parts along dimension 0, may hold values from 1 to 64, 128 in all within a row
- document_adapter: int32 [8, 4], P('groups'), parts along dimension 0, may hold values from 0 to 3, as said below
- adapter_out_row: int32 [8], P('groups'), parts along dimension 0, may hold values from 0 to 3, each once
Outputs:
- input_grad: bfloat16 [1024, 14848], P(('groups', 'tensor'), 'dp'), parts along dimension 0
- grad_down: float32 [8, 64, 14848], P(('groups', 'dp'), None, 'tensor'), parts along dimension 0
- grad_up: float32 [8, 64, 15872], P(('groups', 'dp'), None, 'tensor'), parts along dimension 0
There are 2 independent parts, one for each index of `groups`. A program takes and returns all parts, laid end to end along the dimension named above; an argument that names none is the same for every part. Nothing has to cross between parts.
Inputs may be any that keep to these rules, and one draw needn't show every extreme that they name: `document_lengths`: each row holds the lengths of the 4 documents packed in order into one block of 128 tokens; a row sums to 128. `document_adapter`: the adapter of each document; the 4 documents of one block have distinct adapters. `adapter_out_row`: a permutation; row adapter_out_row[a] of the gradients belongs to adapter a and is owned by index adapter_out_row[a] // 1 of dp.
All inputs are finite; a program needn't handle non-finite values.
Results may differ from a plain program's by a relative error of at most 0.017.
Values may be sent and summed in bfloat16 or wider, within the bound.
A program may use at most 192 MiB of HBM per device.

v0:
```python
import jax
import jax.numpy as jnp
from jax import lax
from jax.sharding import PartitionSpec as P

BLK = 64


adapter_gain = 2.0


def token_adapters(document_lengths, document_adapter, tok_dev):
    ends = jnp.cumsum(document_lengths, axis=1)
    starts = ends - document_lengths
    position = jnp.arange(tok_dev, dtype=jnp.int32)
    inside = (starts[:, :, None] <= position[None, None, :]) & (
        position[None, None, :] < ends[:, :, None]
    )
    chosen = jnp.sum(jnp.where(inside, document_adapter[:, :, None], 0), axis=1)
    return chosen.reshape(-1)


def slot_lookup(labels, adapter_out_row):
    count = adapter_out_row.shape[0]
    match = labels[:, None] == jnp.arange(count, dtype=jnp.int32)[None, :]
    return jnp.sum(jnp.where(match, adapter_out_row[None, :], 0), axis=1)


def one_hot(labels, count):
    return (labels[:, None] == jnp.arange(count, dtype=jnp.int32)[None, :]).astype(jnp.bfloat16)


def spread_rows(selection, values):
    rows = values.shape[0]
    return (selection[:, :, None] * values[:, None, :]).reshape(
        rows, selection.shape[1] * values.shape[1]
    )


def rank_terms(out_rows, flattened_up, selection, rank_position):
    score_values = jnp.einsum(
        "tn,kn->tk", out_rows, flattened_up, preferred_element_type=jnp.float32
    )
    score_values = score_values.reshape(out_rows.shape[0], selection.shape[1], rank_position)
    return adapter_gain * jnp.sum(score_values * selection.astype(jnp.float32)[:, :, None], axis=1)


def per_device(
    output_gradient,
    saved_layer_input,
    adapter_middle,
    frozen_weight,
    block_row_scale,
    adapter_down_weight,
    adapter_up_weight,
    document_lengths,
    document_adapter,
    adapter_out_row,
):
    tok_dev = output_gradient.shape[0]
    dp_index = lax.axis_index("dp")
    tp_index = lax.axis_index("tensor")
    tp_count = lax.axis_size("tensor")
    adapter_list = adapter_up_weight.shape[0]
    rank_position = adapter_up_weight.shape[1]
    labels = token_adapters(document_lengths, document_adapter, tok_dev)
    slots = slot_lookup(labels, adapter_out_row)
    selection = one_hot(labels, adapter_list)
    flattened_up = adapter_up_weight.reshape(
        adapter_list * rank_position, adapter_up_weight.shape[2]
    )
    scales = jnp.repeat(block_row_scale, BLK, axis=0)
    weight = (frozen_weight.astype(jnp.float32) * scales).astype(jnp.bfloat16)
    out_all = lax.all_gather(output_gradient, "dp", axis=0, tiled=True)
    all_terms = rank_terms(out_all, flattened_up, selection, rank_position)
    middle_gradient = lax.psum(all_terms.astype(jnp.bfloat16), "tensor")
    share = out_all.shape[0] // tp_count
    summed = lax.psum_scatter(
        jnp.einsum("tn,dn->td", out_all, weight, preferred_element_type=jnp.float32).astype(
            jnp.bfloat16
        ),
        "tensor",
        scatter_dimension=0,
        tiled=True,
    ).astype(jnp.float32)
    first_row = tp_index * share
    mid_rows_here = lax.dynamic_slice_in_dim(middle_gradient, first_row, share, 0)
    pick_rows = lax.dynamic_slice_in_dim(selection, first_row, share, 0)
    flattened_down = adapter_down_weight.reshape(
        adapter_list * rank_position, adapter_down_weight.shape[2]
    )
    adapter_contribution = jnp.dot(
        spread_rows(pick_rows, mid_rows_here), flattened_down, preferred_element_type=jnp.float32
    )
    input_grad = (summed + adapter_contribution).astype(jnp.bfloat16)
    own_slots = lax.dynamic_slice_in_dim(slots, dp_index * tok_dev, tok_dev, 0)
    own_mid = lax.dynamic_slice_in_dim(middle_gradient, dp_index * tok_dev, tok_dev, 0)
    slot_selection = one_hot(own_slots, adapter_list)
    down_part = jnp.einsum(
        "tk,td->kd",
        spread_rows(slot_selection, own_mid),
        saved_layer_input,
        preferred_element_type=jnp.float32,
    )
    up_portion = adapter_gain * jnp.einsum(
        "me,mr->er",
        spread_rows(slot_selection, adapter_middle),
        output_gradient,
        preferred_element_type=jnp.float32,
    )
    down_part = down_part.reshape(adapter_list, rank_position, -1)
    up_portion = up_portion.reshape(adapter_list, rank_position, -1)
    grad_down, grad_up = (
        lax.psum_scatter(
            down_part.astype(jnp.bfloat16), "dp", scatter_dimension=0, tiled=True
        ).astype(jnp.float32),
        lax.psum_scatter(
            up_portion.astype(jnp.bfloat16), "dp", scatter_dimension=0, tiled=True
        ).astype(jnp.float32),
    )
    return (input_grad, grad_down, grad_up)


def solution(mesh):
    placed = (
        P(("groups", "dp"), "tensor"),
        P(("groups", "dp"), "tensor"),
        P(("groups", "dp"), None),
        P("dp", "tensor"),
        P("dp", "tensor"),
        P("groups", None, "dp"),
        P("groups", None, "tensor"),
        P("groups", None),
        P("groups", None),
        P("groups"),
    )
    return jax.shard_map(
        per_device,
        mesh=mesh,
        in_specs=placed,
        out_specs=(
            P(("groups", "tensor"), "dp"),
            P(("groups", "dp"), None, "tensor"),
            P(("groups", "dp"), None, "tensor"),
        ),
        check_vma=False,
    )
```

profile of v0, /device:TPU:3, one launch (start us, length us, event | category | flops | bytes accessed | tf_op | source)
XLA Modules:
  0.0 262.8 jit_solution(15930417032929059061)
XLA Ops:
  7.2 0.0 copy-start
  7.2 0.0 all-gather.2.cloned.1.call-start
  7.2 0.7 all-gather.2.cloned.1.call-update
  7.9 0.0 all-reduce.2.cloned.1.call-start
  8.0 0.9 reduce_window_sum.11
  8.8 0.7 sub.3
  9.5 0.8 select_reduce_fusion.1
  10.3 0.7 select_reduce_fusion
  11.0 0.1 dynamic_slice.14
  11.1 0.7 broadcast_multiply_fusion
  11.8 77.6 %all-gather.2.cloned.1.call-done = bf16[512,3968]{1,0:T(8,128)(2,1)} async-done(((bf16[128,3968]{1,0:T(8,128)(2,1)}), bf16[512,3968]{1,0:T(8,128)(2,1)}) %all-gather.2.cloned.1.call-update) | async-done | bytes 4063248 | tf_op jit(solution)/shard_map/all_gather | solution.py:74
  89.5 0.0 copy-done
  89.5 0.0 copy-start.2
  89.5 3.5 %fusion.10 = f32[512,64]{0,1:T(8,128)S(1)} fusion(bf16[4,64,3968]{2,1,0:T(8,128)(2,1)S(1)} %copy-done, bf16[512,3968]{1,0:T(8,128)(2,1)} %all-gather.2.cloned.1.call-done, f32[512,4]{0,1:T(4,128)S(1)} %get-tuple-element.9), kind=kOutput, calls=%fused_computation.13 | convolution fusion | flops 1040416768 | bytes 6234112 | tf_op jit(solution)/shard_map/tn,kn->tk/dot_general | solution.py:41
  93.0 0.0 copy-start.4
  93.0 0.6 multiply_convert_fusion
  93.6 0.0 all-reduce.2.cloned.1.call-update
  93.7 0.0 reduce-scatter.8.cloned.1.call-start
  93.7 0.0 copy-done.2
  93.7 2.0 fusion.2
  95.7 0.0 copy-start.3
  95.7 0.0 reduce-scatter.8.cloned.1.call-update
  95.7 0.0 reduce-scatter.6.cloned.1.call-start
  95.8 26.0 %all-reduce.2.cloned.1.call-done = bf16[512,64]{0,1:T(8,128)(2,1)} async-done(((bf16[512,64]{0,1:T(8,128)(2,1)}), bf16[512,64]{0,1:T(8,128)(2,1)}) %all-reduce.2.cloned.1.call-update) | async-done | bytes 65552 | tf_op jit(solution)/shard_map/psum | solution.py:76
  121.8 0.7 constant_dynamic-slice_fusion
  122.5 0.0 copy-done.4
  122.5 1.9 convolution_convert_fusion.1
  124.4 0.0 reduce-scatter.6.cloned.1.call-update
  124.4 0.0 reduce-scatter.10.cloned.1.call-start
  124.5 0.0 copy-done.3
  124.5 20.5 %fusion = bf16[3712,3968]{1,0:T(8,128)(2,1)} fusion(bf16[3712,3968]{1,0:T(8,128)(2,1)} %param.13, f32[58,3968]{1,0:T(8,128)S(1)} %copy-done.3), kind=kLoop, calls=%fused_computation.1 | loop fusion | flops 44187648 | bytes 59837440 | tf_op jit(solution)/shard_map/convert_element_type | solution.py:73
  145.1 22.6 %fusion.1 = bf16[512,3712]{0,1:T(8,128)(2,1)} fusion(bf16[3712,3968]{1,0:T(8,128)(2,1)} %fusion, bf16[512,3968]{1,0:T(8,128)(2,1)} %all-gather.2.cloned.1.call-done), kind=kOutput, calls=%fused_computation.4 | convolution fusion | flops 15084617728 | bytes 37322752 | tf_op jit(solution)/shard_map/tn,dn->td/dot_general | solution.py:79
  167.7 6.2 %copy.17 = bf16[512,3712]{1,0:T(8,128)(2,1)} copy(bf16[512,3712]{0,1:T(8,128)(2,1)} %fusion.1) | data formatting | bytes 7602176
  173.9 0.0 reduce-scatter.10.cloned.1.call-update
  173.9 0.0 copy-start.1
  174.0 0.0 reduce-scatter.8.cloned.1.call-done
  174.0 2.2 convert_element_type.71
  176.2 33.9 %reduce-scatter.6.cloned.1.call-done = bf16[1,64,3712]{2,1,0:T(8,128)(2,1)} async-done(((bf16[4,64,3712]{2,1,0:T(8,128)(2,1)}), bf16[1,64,3712]{2,1,0:T(8,128)(2,1)}) %reduce-scatter.6.cloned.1.call-update) | async-done | bytes 475152 | tf_op jit(solution)/shard_map/reduce_scatter | solution.py:114
  210.1 2.0 convert_element_type.68
  212.1 41.0 %reduce-scatter.10.cloned.1.call-done = bf16[128,3712]{1,0:T(8,128)(2,1)} async-done(((bf16[512,3712]{1,0:T(8,128)(2,1)}), bf16[128,3712]{1,0:T(8,128)(2,1)}) %reduce-scatter.10.cloned.1.call-update) | async-done | bytes 950288 | tf_op jit(solution)/shard_map/reduce_scatter | solution.py:78
  253.2 3.2 %fusion.4 = bf16[128,3712]{1,0:T(8,128)(2,1)} fusion(bf16[4,64,3712]{2,1,0:T(8,128)(2,1)} %param.15, bf16[128,3712]{1,0:T(8,128)(2,1)} %reduce-scatter.10.cloned.1.call-done, bf16[128,64]{0,1:T(8,128)(2,1)S(1)} %get-tuple-element.7, bf16[128,4]{0,1:T(4,128)(2,1)S(1)} %constant_dynamic-slice_fusion.2), kind=kOutput, calls=%fused_computation.9 | convolution fusion | flops 244727808 | bytes 3818496 | tf_op jit(solution)/shard_map/dot_general | solution.py:92
  256.3 0.0 copy-done.1
  (3 shorter events, 0.0 us)
Async XLA Ops:
  7.2 82.3 %copy-start = (bf16[4,64,3968]{2,1,0:T(8,128)(2,1)S(1)}, bf16[4,64,3968]{2,1,0:T(8,128)(2,1)}, u32[]{:S(2)}) copy-start(bf16[4,64,3968]{2,1,0:T(8,128)(2,1)} %param.16) | copy-start | bytes 6094852
  7.2 82.3 %all-gather.2.cloned.1.call-start = ((), (), s32[]{:S(2)}) async-start(), calls=%async_computation.3 | async-start | bytes 5079040 | tf_op jit(solution)/shard_map/all_gather | solution.py:74
  7.9 113.9 %all-reduce.2.cloned.1.call-start = ((), (), s32[]{:S(2)}) async-start(), calls=%async_computation.4 | async-start | bytes 131072 | tf_op jit(solution)/shard_map/psum | solution.py:76
  89.5 4.3 %copy-start.2 = (bf16[128,3968]{1,0:T(8,128)(2,1)S(1)}, bf16[128,3968]{1,0:T(8,128)(2,1)}, u32[]{:S(2)}) copy-start(bf16[128,3968]{1,0:T(8,128)(2,1)} %param.10) | copy-start | bytes 3047428
  93.0 29.5 %copy-start.4 = (bf16[128,3712]{1,0:T(8,128)(2,1)S(1)}, bf16[128,3712]{1,0:T(8,128)(2,1)}, u32[]{:S(2)}) copy-start(bf16[128,3712]{1,0:T(8,128)(2,1)} %param.11) | copy-start | bytes 2850820
  93.7 80.3 %reduce-scatter.8.cloned.1.call-start = ((), (), s32[]{:S(2)}) async-start(), calls=%async_computation.6 | async-start | bytes 2539520 | tf_op jit(solution)/shard_map/reduce_scatter | solution.py:117
  95.7 28.8 %copy-start.3 = (f32[58,3968]{1,0:T(8,128)S(1)}, f32[58,3968]{1,0:T(8,128)}, u32[]{:S(2)}) copy-start(f32[58,3968]{1,0:T(8,128)} %param.14) | copy-start | bytes 2761732
  95.7 114.4 %reduce-scatter.6.cloned.1.call-start = ((), (), s32[]{:S(2)}) async-start(), calls=%async_computation.5 | async-start | bytes 2375680 | tf_op jit(solution)/shard_map/reduce_scatter | solution.py:114
  124.4 128.7 %reduce-scatter.10.cloned.1.call-start = ((), (), s32[]{:S(2)}) async-start(), calls=%async_computation.7 | async-start | bytes 4751360 | tf_op jit(solution)/shard_map/reduce_scatter | solution.py:78
  173.9 82.4 %copy-start.1 = (bf16[4,64,3968]{2,1,0:T(8,128)(2,1)S(1)}, bf16[4,64,3968]{2,1,0:T(8,128)(2,1)}, u32[]{:S(2)}) copy-start(bf16[4,64,3968]{2,1,0:T(8,128)(2,1)} %param.16) | copy-start | bytes 6094852
Sparse Core Ops, SparseCore 0:
  9.6 79.8 all-gather.1
  93.8 27.9 all-reduce.1
  124.2 43.9 reduce-scatter.7
  170.4 39.6 reduce-scatter.5
  212.7 40.4 reduce-scatter.9
where the time goes:
time: 266 us; the launch traced here: 263 us
  waiting for transfers between devices  179 us (67%)
  matrix products  33.2 us (12%)
  other arithmetic  29.2 us (11%)
  between operations  13.9 us (5%)
  local copies, waits for them, and re-layouts  7.08 us (3%)
    all_gather x1, waiting for transfers between devices, per_device(): out_all = lax.all_gather(output_gradient, 'dp', axis=0, tiled=True)  77.6 us
    reduce_scatter x1, waiting for transfers between devices, per_device(): lax.psum_scatter(jnp.einsum('tn,dn->td', out_all, weight, preferred_eleme...  41 us
    reduce_scatter x1, waiting for transfers between devices, per_device(): lax.psum_scatter(down_part.astype(jnp.bfloat16), 'dp', scatter_dimension=...  33.9 us
    psum x1, waiting for transfers between devices, per_device(): middle_gradient = lax.psum(all_terms.astype(jnp.bfloat16), 'tensor')  26 us
    dot_general x1, matrix products, per_device(): jnp.einsum('tn,dn->td', out_all, weight, preferred_element_type=jnp.float32)  22.6 us
    convert_element_type x1, other arithmetic, per_device(): weight = (frozen_weight.astype(jnp.float32) * scales).astype(jnp.bfloat16)  20.5 us
    unnamed x11, local copies, waits for them, and re-layouts  6.26 us
  transfers between devices with their start and end apart: 5, of which 4 were waited for; matrix products, arithmetic and copies ran while one was open for 24% of the time, Pallas kernels for 0%

commit v1 on v0

--- a/solution.py
+++ b/solution.py
@@ -1,9 +1,506 @@
+import functools
+
 import jax
 import jax.numpy as jnp
 from jax import lax
+from jax.experimental import pallas as pl
+from jax.experimental.pallas import tpu as pltpu
 from jax.sharding import PartitionSpec as P
 
+MESH = pl.DeviceIdType.MESH
 BLK = 64
+PIECE = 128
+F32 = jnp.float32
+BF16 = jnp.bfloat16
+
+
+def spans(total, step):
+    return [(s, min(step, total - s)) for s in range(0, total, step)]
+
+
+def tiled(total, step, body):
+    full = total // step
+
+    def run(j, carry):
+        body(pl.multiple_of(j * step, 128), step)
+        return carry
+
+    lax.fori_loop(0, full, run, 0)
+    if total % step:
+        body(full * step, total % step)
+
+
+def dot_nt(a, b):
+    return lax.dot_general(a, b, (((1,), (1,)), ((), ())), preferred_element_type=F32)
+
+
+def fused(
+    n,
+    len_s, doc_s, row_s,
+    g_h, x_h, mid_h, w_h, sc_h, dn_h, up_h,
+    out_h, gd_h, gu_h,
+    gall, w, sc, x, dn, up, mid, at, mpart, mrecv, sacc, acc, psend, precv, part, rsrecv, gu, gd,
+    loc, wsem, ag_s, ag_r, a_s, a_r, m_s, m_r, rs_s, rs_r, p_s, p_r,
+):
+    z = lax.axis_index("dp")
+    t = lax.axis_index("tensor")
+    tok, kdim = g_h.shape
+    ndim = x_h.shape[1]
+    ranks = up_h.shape[0]
+    rank = mid_h.shape[1]
+    shift = rank.bit_length() - 1
+    pieces = w_h.shape[0] // PIECE
+    chunks = spans(kdim, 1024)
+
+    loads = [
+        pltpu.make_async_copy(src, dst, loc.at[i])
+        for i, (src, dst) in enumerate(
+            [(g_h, gall.at[z]), (up_h, up), (mid_h, mid), (sc_h, sc), (x_h, x), (dn_h, dn)]
+        )
+    ]
+    for copy in loads:
+        copy.start()
+
+    def w_copy(i):
+        rows = pl.ds(pl.multiple_of(i * PIECE, PIECE), PIECE)
+        return pltpu.make_async_copy(w_h.at[rows], w.at[rows], wsem.at[i])
+
+    def start_w(i, carry):
+        w_copy(i).start()
+        return carry
+
+    lax.fori_loop(0, pieces, start_w, 0)
+
+    barrier = pltpu.get_barrier_semaphore()
+    for d in range(1, n):
+        pl.semaphore_signal(barrier, inc=1, device_id={"dp": lax.rem(z + d, n)}, device_id_type=MESH)
+        pl.semaphore_signal(barrier, inc=1, device_id={"tensor": lax.rem(t + d, n)}, device_id_type=MESH)
+    pl.semaphore_wait(barrier, 2 * (n - 1))
+
+    def ag(direction, b, c):
+        first, width = chunks[c]
+        ref = gall.at[b, :, pl.ds(first, width)]
+        return pltpu.make_async_remote_copy(
+            src_ref=ref,
+            dst_ref=ref,
+            send_sem=ag_s.at[direction, b, c],
+            recv_sem=ag_r.at[b, c],
+            device_id={"dp": z + 1 if direction == 0 else z - 1},
+            device_id_type=MESH,
+        )
+
+    loads[0].wait()
+    for c in range(len(chunks)):
+
+        @pl.when(z < n - 1)
+        def _():
+            ag(0, z, c).start()
+
+        @pl.when(z > 0)
+        def _():
+            ag(1, z, c).start()
+
+    def doc_values(b, position, pick):
+        total = jnp.zeros(position.shape, jnp.int32)
+        begin = jnp.int32(0)
+        for s in range(len_s.shape[1]):
+            end = begin + len_s[b, s]
+            inside = (position >= begin) & (position < end)
+            total = total + jnp.where(inside, pick(b, s), 0)
+            begin = end
+        return total
+
+    def adapter_of(b, s):
+        return doc_s[b, s]
+
+    def slot_of(b, s):
+        a = doc_s[b, s]
+        found = jnp.int32(0)
+        for i in range(row_s.shape[0]):
+            found = found + jnp.where(a == i, row_s[i], 0)
+        return found
+
+    row_id = lax.broadcasted_iota(jnp.int32, (tok, ranks), 0)
+    col_group = lax.broadcasted_iota(jnp.int32, (tok, ranks), 1) >> shift
+
+    def masked_scores(b, score):
+        keep = doc_values(b, row_id, adapter_of) == col_group
+        return jnp.where(keep, 2.0 * score, 0.0).astype(BF16)
+
+    loads[2].wait()
+    at[z] = mid[...].astype(F32).T.astype(BF16)
+
+    def a_copy(d):
+        return pltpu.make_async_remote_copy(
+            src_ref=at.at[z],
+            dst_ref=at.at[z],
+            send_sem=a_s.at[d - 1],
+            recv_sem=a_r.at[z],
+            device_id={"dp": lax.rem(z + d, n)},
+            device_id_type=MESH,
+        )
+
+    def a_wait(b):
+        pltpu.make_async_remote_copy(
+            src_ref=at.at[b], dst_ref=at.at[b], send_sem=a_s.at[0], recv_sem=a_r.at[b],
+            device_id={"dp": lax.rem(z + 1, n)}, device_id_type=MESH,
+        ).wait_recv()
+
+    for d in range(1, n):
+        a_copy(d).start()
+
+    loads[1].wait()
+    own_score = dot_nt(gall[z], up[...])
+    mpart[...] = masked_scores(z, own_score)
+
+    def m_copy(d):
+        return pltpu.make_async_remote_copy(
+            src_ref=mpart,
+            dst_ref=mrecv.at[d - 1],
+            send_sem=m_s.at[d - 1],
+            recv_sem=m_r.at[d - 1],
+            device_id={"tensor": lax.rem(t + d, n)},
+            device_id_type=MESH,
+        )
+
+    for d in range(1, n):
+        m_copy(d).start()
+
+    loads[3].wait()
+
+    def scale_w(i, carry):
+        w_copy(i).wait()
+        for h in range(PIECE // BLK):
+            rows = pl.ds(pl.multiple_of(i * PIECE + h * BLK, BLK), BLK)
+            for first, width in spans(kdim, 512):
+                cols = pl.ds(first, width)
+                factor = sc[pl.ds(i * (PIECE // BLK) + h, 1), cols]
+                w[rows, cols] = (w[rows, cols].astype(F32) * factor).astype(BF16)
+        return carry
+
+    lax.fori_loop(0, pieces // 3, scale_w, 0)
+
+    for d in range(1, n):
+        m_copy(d).wait_recv()
+    total = mpart[...].astype(F32)
+    for d in range(1, n):
+        total = total + mrecv[d - 1].astype(F32)
+    same = (
+        lax.broadcasted_iota(jnp.int32, (ranks, ranks), 0) & (rank - 1)
+    ) == (lax.broadcasted_iota(jnp.int32, (ranks, ranks), 1) & (rank - 1))
+    copies = jnp.dot(
+        total.astype(BF16), jnp.where(same, 1.0, 0.0).astype(BF16), preferred_element_type=F32
+    )
+    slot_mask = doc_values(z, row_id, slot_of) == col_group
+    by_slot = jnp.where(slot_mask, copies, 0.0).T.astype(BF16)
+    loads[4].wait()
+
+    def down_tile(first, width):
+        cols = pl.ds(first, width)
+        value = jnp.dot(by_slot, x[:, cols], preferred_element_type=F32).astype(BF16)
+        for k in range(n):
+            part[k, :, cols] = value[k * rank:(k + 1) * rank]
+
+    tiled(ndim, 512, down_tile)
+
+    def rs(direction, k):
+        if direction == 0:
+            place, target = k, z + 1
+        else:
+            place, target = jnp.where(k == z - 1, n, k), z - 1
+        return pltpu.make_async_remote_copy(
+            src_ref=part.at[k],
+            dst_ref=rsrecv.at[place],
+            send_sem=rs_s.at[k],
+            recv_sem=rs_r.at[place],
+            device_id={"dp": target},
+            device_id_type=MESH,
+        )
+
+    def rs_wait(place):
+        pltpu.make_async_remote_copy(
+            src_ref=part.at[0], dst_ref=rsrecv.at[place], send_sem=rs_s.at[0],
+            recv_sem=rs_r.at[place], device_id={"dp": lax.rem(z + 1, n)}, device_id_type=MESH,
+        ).wait_recv()
+
+    def rs_add(place, k):
+        rs_wait(place)
+
+        def add(first, width):
+            cols = pl.ds(first, width)
+            part[k, :, cols] = (
+                part[k, :, cols].astype(F32) + rsrecv[place, :, cols].astype(F32)
+            ).astype(BF16)
+
+        tiled(ndim, 512, add)
+
+    for k in range(n - 1, 0, -1):
+
+        @pl.when(z == 0)
+        def _():
+            rs(0, k).start()
+
+        @pl.when(z == n - 1)
+        def _():
+            rs(1, n - 1 - k).start()
+
+    lax.fori_loop(pieces // 3, pieces, scale_w, 0)
+
+    def multiply(b, c, lane):
+        first, width = chunks[c]
+        cols = pl.ds(first, width)
+        rows = gall[b, :, cols]
+        score = dot_nt(rows, up[:, cols])
+        sacc[lane] = score if c == 0 else sacc[lane] + score
+
+        def tile(begin, size):
+            here = pl.ds(begin, size)
+            value = dot_nt(rows, w[here, cols])
+            acc[lane, :, here] = value if c == 0 else acc[lane, :, here] + value
+
+        tiled(ndim, 512, tile)
+
+    def p_copy(b):
+        rel = lax.rem(t - b - 1 + 2 * n, n)
+        return pltpu.make_async_remote_copy(
+            src_ref=psend.at[b],
+            dst_ref=precv.at[rel],
+            send_sem=p_s.at[b],
+            recv_sem=p_r.at[rel],
+            device_id={"tensor": b},
+            device_id_type=MESH,
+        )
+
+    def finish(b, lane):
+        picked = masked_scores(b, sacc[lane])
+
+        def tile(begin, size):
+            here = pl.ds(begin, size)
+            value = acc[lane, :, here] + jnp.dot(picked, dn[:, here], preferred_element_type=F32)
+            psend[b, :, here] = value.astype(BF16)
+
+        tiled(ndim, 512, tile)
+
+        @pl.when(b != t)
+        def _():
+            p_copy(b).start()
+
+    lane_id = lax.broadcasted_iota(jnp.int32, (rank, tok), 1)
+
+    def up_terms(b, fresh):
+        mine = doc_values(b, lane_id, slot_of) == z
+        held = jnp.where(mine, 2.0 * at[b].astype(F32), 0.0).astype(BF16)
+
+        def tile(begin, size):
+            here = pl.ds(begin, size)
+            value = jnp.dot(held, gall[b, :, here], preferred_element_type=F32)
+            value = value.astype(BF16).astype(F32)
+            gu[:, here] = value if fresh else gu[:, here] + value
+
+        tiled(kdim, 512, tile)
+
+    loads[5].wait()
+    for c in range(len(chunks)):
+        multiply(z, c, 0)
+    finish(z, 0)
+    up_terms(z, True)
+
+    def round_step(s, carry):
+        low, high = z - s, z + s
+        for c in range(len(chunks)):
+
+            @pl.when(low >= 0)
+            def _():
+                ag(0, low, c).wait_recv()
+
+                @pl.when(z < n - 1)
+                def _():
+                    ag(0, low, c).start()
+
+            @pl.when(high < n)
+            def _():
+                ag(1, high, c).wait_recv()
+
+                @pl.when(z > 0)
+                def _():
+                    ag(1, high, c).start()
+
+            @pl.when(low >= 0)
+            def _():
+                multiply(low, c, 0)
+
+            @pl.when(high < n)
+            def _():
+                multiply(high, c, 1)
+
+        @pl.when(low >= 0)
+        def _():
+            finish(low, 0)
+            a_wait(low)
+            up_terms(low, False)
+
+        @pl.when(high < n)
+        def _():
+            finish(high, 1)
+            a_wait(high)
+            up_terms(high, False)
+
+        up_slot = z + n - 1 - s
+
+        @pl.when((z > 0) & (up_slot < n) & (up_slot > z))
+        def _():
+            rs_add(up_slot, up_slot)
+            rs(0, up_slot).start()
+
+        down_slot = z - (n - 1) + s
+
+        @pl.when((z < n - 1) & (down_slot >= 0) & (down_slot < z))
+        def _():
+            rs_add(down_slot, down_slot)
+            rs(1, down_slot).start()
+
+        return carry
+
+    lax.fori_loop(1, n, round_step, 0)
+    write_up = pltpu.make_async_copy(gu, gu_h, loc.at[0])
+    write_up.start()
+
+    @pl.when(z > 0)
+    def _():
+        rs_wait(z)
+
+    @pl.when(z < n - 1)
+    def _():
+        rs_wait(n)
+
+    @pl.when(z == 0)
+    def _():
+        gd[...] = part[z].astype(F32) + rsrecv[n].astype(F32)
+
+    @pl.when(z == n - 1)
+    def _():
+        gd[...] = part[z].astype(F32) + rsrecv[z].astype(F32)
+
+    @pl.when((z > 0) & (z < n - 1))
+    def _():
+        gd[...] = part[z].astype(F32) + rsrecv[z].astype(F32) + rsrecv[n].astype(F32)
+
+    write_down = pltpu.make_async_copy(gd, gd_h, loc.at[1])
+    write_down.start()
+
+    for rel in range(n - 1):
+        pltpu.make_async_remote_copy(
+            src_ref=psend.at[0], dst_ref=precv.at[rel], send_sem=p_s.at[0], recv_sem=p_r.at[rel],
+            device_id={"tensor": lax.rem(t + 1, n)}, device_id_type=MESH,
+        ).wait_recv()
+
+    def out_tile(begin, size):
+        here = pl.ds(begin, size)
+        value = psend[t, :, here].astype(F32)
+        for rel in range(n - 1):
+            value = value + precv[rel, :, here].astype(F32)
+        psend[t, :, here] = value.astype(BF16)
+
+    tiled(ndim, 512, out_tile)
+    write_out = pltpu.make_async_copy(psend.at[t], out_h, loc.at[2])
+    write_out.start()
+
+    for d in range(1, n):
+        a_copy(d).wait_send()
+        m_copy(d).wait_send()
+    for b in range(n):
+        for c in range(len(chunks)):
+
+            @pl.when((z < n - 1) & (b <= z))
+            def _():
+                ag(0, b, c).wait_send()
+
+            @pl.when((z > 0) & (b >= z))
+            def _():
+                ag(1, b, c).wait_send()
+
+        @pl.when(b > z)
+        def _():
+            rs(0, b).wait_send()
+
+        @pl.when(b < z)
+        def _():
+            rs(1, b).wait_send()
+
+        @pl.when(b != t)
+        def _():
+            p_copy(b).wait_send()
+
+    write_up.wait()
+    write_down.wait()
+    write_out.wait()
+
+
+def fused_device(n, out_grad, saved, middle, weight, scale, down, up, lengths, adapters, rows):
+    tok, kdim = out_grad.shape
+    ndim = saved.shape[1]
+    count, rank, _ = up.shape
+    ranks = count * rank
+    chunks = len(spans(kdim, 1024))
+    smem = pl.BlockSpec(memory_space=pltpu.SMEM)
+    hbm = pl.BlockSpec(memory_space=pl.ANY)
+    dma = pltpu.SemaphoreType.DMA
+    out, gd, gu = pl.pallas_call(
+        functools.partial(fused, n),
+        out_shape=(
+            jax.ShapeDtypeStruct((tok, ndim), BF16),
+            jax.ShapeDtypeStruct((rank, ndim), F32),
+            jax.ShapeDtypeStruct((rank, kdim), F32),
+        ),
+        in_specs=[smem] * 3 + [hbm] * 7,
+        out_specs=(hbm, hbm, hbm),
+        scratch_shapes=[
+            pltpu.VMEM((n, tok, kdim), BF16),
+            pltpu.VMEM(weight.shape, BF16),
+            pltpu.VMEM(scale.shape, F32),
+            pltpu.VMEM((tok, ndim), BF16),
+            pltpu.VMEM((ranks, ndim), BF16),
+            pltpu.VMEM((ranks, kdim), BF16),
+            pltpu.VMEM((tok, rank), BF16),
+            pltpu.VMEM((n, rank, tok), BF16),
+            pltpu.VMEM((tok, ranks), BF16),
+            pltpu.VMEM((n - 1, tok, ranks), BF16),
+            pltpu.VMEM((2, tok, ranks), F32),
+            pltpu.VMEM((2, tok, ndim), F32),
+            pltpu.VMEM((n, tok, ndim), BF16),
+            pltpu.VMEM((n - 1, tok, ndim), BF16),
+            pltpu.VMEM((n, rank, ndim), BF16),
+            pltpu.VMEM((n + 1, rank, ndim), BF16),
+            pltpu.VMEM((rank, kdim), F32),
+            pltpu.VMEM((rank, ndim), F32),
+            dma((6,)),
+            dma((weight.shape[0] // PIECE,)),
+            dma((2, n, chunks)),
+            dma((n, chunks)),
+            dma((n - 1,)),
+            dma((n,)),
+            dma((n - 1,)),
+            dma((n - 1,)),
+            dma((n,)),
+            dma((n + 1,)),
+            dma((n,)),
+            dma((n - 1,)),
+        ],
+        compiler_params=pltpu.CompilerParams(
+            collective_id=0, has_side_effects=True, vmem_limit_bytes=63 * 1024 * 1024
+        ),
+        cost_estimate=pl.CostEstimate(
+            flops=2 * n * tok * kdim * ndim,
+            bytes_accessed=2 * kdim * ndim,
+            transcendentals=0,
+        ),
+        name="fused_backward",
+    )(
+        lengths, adapters, rows,
+        out_grad, saved, middle, weight, scale,
+        down.reshape(ranks, down.shape[2]), up.reshape(ranks, up.shape[2]),
+    )
+    return out, gd[None], gu[None]
 
 
 adapter_gain = 2.0
@@ -121,6 +618,22 @@
     return (input_grad, grad_down, grad_up)
 
 
+def device_program(n_dp, n_tensor, *operands):
+    out_grad, saved, middle, weight, _, _, up = operands[:7]
+    tok, kdim = out_grad.shape
+    count, rank, _ = up.shape
+    whole_tiles = kdim % 128 == 0 and saved.shape[1] % 128 == 0 and tok % 128 == 0
+    if (
+        n_dp == n_tensor == count
+        and whole_tiles
+        and weight.shape == (saved.shape[1], kdim)
+        and rank == 64
+        and 2 * kdim * saved.shape[1] <= 32 * 1024 * 1024
+    ):
+        return fused_device(n_dp, *operands)
+    return per_device(*operands)
+
+
 def solution(mesh):
     placed = (
         P(("groups", "dp"), "tensor"),
@@ -135,7 +648,7 @@
         P("groups"),
     )
     return jax.shard_map(
-        per_device,
+        functools.partial(device_program, mesh.shape["dp"], mesh.shape["tensor"]),
         mesh=mesh,
         in_specs=placed,
         out_specs=(

time: 266 us -> 130 us (0.49); the launches traced: 263 us -> 130 us
  waiting for transfers between devices: 179 us -> 0 us
  Pallas kernels: 0 us -> 122 us
  matrix products: 33.2 us -> 0 us
  other arithmetic: 29.2 us -> 0 us
  between operations: 13.9 us -> 0.65 us
    pallas_call x0 -> x1, Pallas kernels: none -> 122 us  [fused_device(): pl.pallas_call(functools.partial(fused, n), out_shape=(jax.ShapeDtypeStru...]
    all_gather x1 -> x0, waiting for transfers between devices: 77.6 us -> none  [per_device(): out_all = lax.all_gather(output_gradient, 'dp', axis=0, tiled=True)]
    reduce_scatter x3 -> x0, waiting for transfers between devices: 75 us -> none  [the longest x1 41 us: per_device(): lax.psum_scatter(jnp.einsum('tn,dn->td', out_all, weight, preferred_eleme...]
    dot_general x5 -> x0, matrix products: 33.2 us -> none  [the longest x1 22.6 us: per_device(): jnp.einsum('tn,dn->td', out_all, weight, preferred_element_type=jnp.float32)]
    psum x1 -> x0, waiting for transfers between devices: 26 us -> none  [per_device(): middle_gradient = lax.psum(all_terms.astype(jnp.bfloat16), 'tensor')]
    convert_element_type x6 -> x0, other arithmetic: 25.4 us -> none  [the longest x1 20.5 us: per_device(): weight = (frozen_weight.astype(jnp.float32) * scales).astype(jnp.bfloat16)]
    unnamed x11 -> x6, local copies, waits for them, and re-layouts: 6.26 us -> 6.85 us
  transfers between devices with their start and end apart: 5 -> 0, of which waited for: 4 -> 0; matrix products, arithmetic and copies ran while one was open for 24% -> 0% of each run, Pallas kernels for 0% -> 0%
where the time goes in v1:
time: 130 us
  Pallas kernels  122 us (94%)
  local copies, waits for them, and re-layouts  6.85 us (5%)
    pallas_call x1, Pallas kernels, fused_device(): pl.pallas_call(functools.partial(fused, n), out_shape=(jax.ShapeDtypeStru...  122 us
    unnamed x6, local copies, waits for them, and re-layouts  6.85 us

profile of v1, /device:TPU:3, one launch (start us, length us, event | category | flops | bytes accessed | tf_op | source)
XLA Modules:
  0.0 129.6 jit_solution(18110729529694550461)
XLA Ops:
  0.6 1.4 %copy.13.mid_h = bf16[128,64]{1,0:T(8,128)(2,1)} copy(bf16[128,64]{0,1:T(8,128)(2,1)} %param.12) | data formatting | bytes 32768 | tf_op args[2]
  2.1 122.1 %fused_backward.1 = (bf16[128,3712]{1,0:T(8,128)(2,1)}, f32[64,3712]{1,0:T(8,128)}, f32[64,3968]{1,0:T(8,128)}) custom-call(s32[4,4]{1,0:T(4,128)} %len_s.1, s32[4,4]{1,0:T(4,128)} %doc_s.1, s32[4]{0:T(128)} %row_s.1, bf16[128,3968]{1,0:T(8,128)(2,1)} %g_h.1, bf16[128,3712]{1,0:T(8,128)(2,1)} %x_h.1, bf16[128,64]{1,0:T(8,128)(2,1)} %copy.13.mid_h, ...), custom_call_target="tpu_custom_call" | custom-call | flops 15082717184 | bytes 29458432 | tf_op jit(solution)/shard_map/fused_backward/pallas_call | solution.py:448
  124.1 0.0 copy-start
  124.2 2.3 %copy.17 = bf16[128,3712]{1,0:T(8,128)(2,1)} copy(bf16[128,3712]{1,0:T(8,128)(2,1)} %get-tuple-element.12) | data formatting | bytes 1900544
  126.4 2.2 %copy.18 = f32[1,64,3712]{2,1,0:T(8,128)} copy(f32[1,64,3712]{2,1,0:T(8,128)} %bitcast.5) | data formatting | bytes 1900544
  128.6 0.0 copy-done
  128.6 1.0 copy.19
Async XLA Ops:
  124.1 4.5 %copy-start = (f32[64,3968]{1,0:T(8,128)S(1)}, f32[64,3968]{1,0:T(8,128)}, u32[]{:S(2)}) copy-start(f32[64,3968]{1,0:T(8,128)} %get-tuple-element.8) | copy-start | bytes 3047428

commit v2 on v1

--- a/solution.py
+++ b/solution.py
@@ -39,7 +39,7 @@
     len_s, doc_s, row_s,
     g_h, x_h, mid_h, w_h, sc_h, dn_h, up_h,
     out_h, gd_h, gu_h,
-    gall, w, sc, x, dn, up, mid, at, mpart, mrecv, sacc, acc, psend, precv, part, rsrecv, gu, gd,
+    gall, w, sc, x, dn, dnt, up, mid, at, mpart, mrecv, sacc, acc, psend, precv, part, rsrecv, gu, gd,
     loc, wsem, ag_s, ag_r, a_s, a_r, m_s, m_r, rs_s, rs_r, p_s, p_r,
 ):
     z = lax.axis_index("dp")
@@ -89,14 +89,21 @@
             device_id_type=MESH,
         )
 
+    near = t < n // 2
+    early = len(chunks) // 2
+    hold_up = (z == n - 2) & jnp.logical_not(near)
+    hold_down = (z == 1) & near
+    late = ((z == n - 1) & jnp.logical_not(near)) | ((z == 0) & near)
+
     loads[0].wait()
     for c in range(len(chunks)):
-
-        @pl.when(z < n - 1)
+        now = c < early
+
+        @pl.when((z < n - 1) & (jnp.logical_not(hold_up) | now))
         def _():
             ag(0, z, c).start()
 
-        @pl.when(z > 0)
+        @pl.when((z > 0) & (jnp.logical_not(hold_down) | now))
         def _():
             ag(1, z, c).start()
 
@@ -234,15 +241,13 @@
 
         tiled(ndim, 512, add)
 
-    for k in range(n - 1, 0, -1):
-
-        @pl.when(z == 0)
-        def _():
-            rs(0, k).start()
-
-        @pl.when(z == n - 1)
-        def _():
-            rs(1, n - 1 - k).start()
+    @pl.when(z == 0)
+    def _():
+        rs(0, n - 1).start()
+
+    @pl.when(z == n - 1)
+    def _():
+        rs(1, 0).start()
 
     lax.fori_loop(pieces // 3, pieces, scale_w, 0)
 
@@ -255,10 +260,10 @@
 
         def tile(begin, size):
             here = pl.ds(begin, size)
-            value = dot_nt(rows, w[here, cols])
-            acc[lane, :, here] = value if c == 0 else acc[lane, :, here] + value
-
-        tiled(ndim, 512, tile)
+            value = dot_nt(w[here, cols], rows)
+            acc[lane, here] = value if c == 0 else acc[lane, here] + value
+
+        tiled(ndim, 1280, tile)
 
     def p_copy(b):
         rel = lax.rem(t - b - 1 + 2 * n, n)
@@ -276,8 +281,7 @@
 
         def tile(begin, size):
             here = pl.ds(begin, size)
-            value = acc[lane, :, here] + jnp.dot(picked, dn[:, here], preferred_element_type=F32)
-            psend[b, :, here] = value.astype(BF16)
+            psend[b, here] = (acc[lane, here] + dot_nt(dnt[here], picked)).astype(BF16)
 
         tiled(ndim, 512, tile)
 
@@ -300,68 +304,113 @@
         tiled(kdim, 512, tile)
 
     loads[5].wait()
+
+    def turn(i, carry):
+        here = pl.ds(pl.multiple_of(i * 128, 128), 128)
+        dnt[here] = dn[:, here].astype(F32).T.astype(BF16)
+        return carry
+
+    lax.fori_loop(0, ndim // 128, turn, 0)
     for c in range(len(chunks)):
         multiply(z, c, 0)
     finish(z, 0)
     up_terms(z, True)
 
-    def round_step(s, carry):
+    def chunk_step(s, c, lane_low, lane_high):
         low, high = z - s, z + s
-        for c in range(len(chunks)):
-
-            @pl.when(low >= 0)
+
+        @pl.when(low >= 0)
+        def _():
+            ag(0, low, c).wait_recv()
+
+            @pl.when(z < n - 1)
             def _():
-                ag(0, low, c).wait_recv()
-
-                @pl.when(z < n - 1)
-                def _():
-                    ag(0, low, c).start()
-
-            @pl.when(high < n)
+                ag(0, low, c).start()
+
+        @pl.when(high < n)
+        def _():
+            ag(1, high, c).wait_recv()
+
+            @pl.when(z > 0)
             def _():
-                ag(1, high, c).wait_recv()
-
-                @pl.when(z > 0)
-                def _():
-                    ag(1, high, c).start()
-
-            @pl.when(low >= 0)
-            def _():
-                multiply(low, c, 0)
-
-            @pl.when(high < n)
-            def _():
-                multiply(high, c, 1)
+                ag(1, high, c).start()
 
         @pl.when(low >= 0)
         def _():
-            finish(low, 0)
+            multiply(low, c, lane_low)
+
+        @pl.when(high < n)
+        def _():
+            multiply(high, c, lane_high)
+
+    def close_step(s, lane_low, lane_high):
+        low, high = z - s, z + s
+
+        @pl.when(low >= 0)
+        def _():
+            finish(low, lane_low)
             a_wait(low)
             up_terms(low, False)
 
         @pl.when(high < n)
         def _():
-            finish(high, 1)
+            finish(high, lane_high)
             a_wait(high)
             up_terms(high, False)
 
+    def round_step(s, carry):
+        held = late & (s == 1)
+        low_lane = jnp.where(held, 1, 0)
+        high_lane = jnp.where(late & (s > 1), 0, 1)
+        for c in range(early):
+            chunk_step(s, c, low_lane, high_lane)
+
+        @pl.when(jnp.logical_not(held))
+        def _():
+            for c in range(early, len(chunks)):
+                chunk_step(s, c, low_lane, high_lane)
+            close_step(s, low_lane, high_lane)
+
+        @pl.when(hold_up & (s == n - 2))
+        def _():
+            for c in range(early, len(chunks)):
+                ag(0, z, c).start()
+
+        @pl.when(hold_down & (s == n - 2))
+        def _():
+            for c in range(early, len(chunks)):
+                ag(1, z, c).start()
+
         up_slot = z + n - 1 - s
 
-        @pl.when((z > 0) & (up_slot < n) & (up_slot > z))
-        def _():
-            rs_add(up_slot, up_slot)
+        @pl.when((up_slot < n) & (up_slot > z))
+        def _():
+            @pl.when(z > 0)
+            def _():
+                rs_add(up_slot, up_slot)
+
             rs(0, up_slot).start()
 
         down_slot = z - (n - 1) + s
 
-        @pl.when((z < n - 1) & (down_slot >= 0) & (down_slot < z))
-        def _():
-            rs_add(down_slot, down_slot)
+        @pl.when((down_slot >= 0) & (down_slot < z))
+        def _():
+            @pl.when(z < n - 1)
+            def _():
+                rs_add(down_slot, down_slot)
+
             rs(1, down_slot).start()
 
         return carry
 
     lax.fori_loop(1, n, round_step, 0)
+
+    @pl.when(late)
+    def _():
+        for c in range(early, len(chunks)):
+            chunk_step(1, c, 1, 1)
+        close_step(1, 1, 1)
+
     write_up = pltpu.make_async_copy(gu, gu_h, loc.at[0])
     write_up.start()
 
@@ -396,10 +445,10 @@
 
     def out_tile(begin, size):
         here = pl.ds(begin, size)
-        value = psend[t, :, here].astype(F32)
+        value = psend[t, here].astype(F32)
         for rel in range(n - 1):
-            value = value + precv[rel, :, here].astype(F32)
-        psend[t, :, here] = value.astype(BF16)
+            value = value + precv[rel, here].astype(F32)
+        psend[t, here] = value.astype(BF16)
 
     tiled(ndim, 512, out_tile)
     write_out = pltpu.make_async_copy(psend.at[t], out_h, loc.at[2])
@@ -448,7 +497,7 @@
     out, gd, gu = pl.pallas_call(
         functools.partial(fused, n),
         out_shape=(
-            jax.ShapeDtypeStruct((tok, ndim), BF16),
+            jax.ShapeDtypeStruct((ndim, tok), BF16),
             jax.ShapeDtypeStruct((rank, ndim), F32),
             jax.ShapeDtypeStruct((rank, kdim), F32),
         ),
@@ -460,15 +509,16 @@
             pltpu.VMEM(scale.shape, F32),
             pltpu.VMEM((tok, ndim), BF16),
             pltpu.VMEM((ranks, ndim), BF16),
+            pltpu.VMEM((ndim, ranks), BF16),
             pltpu.VMEM((ranks, kdim), BF16),
             pltpu.VMEM((tok, rank), BF16),
             pltpu.VMEM((n, rank, tok), BF16),
             pltpu.VMEM((tok, ranks), BF16),
             pltpu.VMEM((n - 1, tok, ranks), BF16),
             pltpu.VMEM((2, tok, ranks), F32),
-            pltpu.VMEM((2, tok, ndim), F32),
-            pltpu.VMEM((n, tok, ndim), BF16),
-            pltpu.VMEM((n - 1, tok, ndim), BF16),
+            pltpu.VMEM((2, ndim, tok), F32),
+            pltpu.VMEM((n, ndim, tok), BF16),
+            pltpu.VMEM((n - 1, ndim, tok), BF16),
             pltpu.VMEM((n, rank, ndim), BF16),
             pltpu.VMEM((n + 1, rank, ndim), BF16),
             pltpu.VMEM((rank, kdim), F32),
@@ -500,7 +550,7 @@
         out_grad, saved, middle, weight, scale,
         down.reshape(ranks, down.shape[2]), up.reshape(ranks, up.shape[2]),
     )
-    return out, gd[None], gu[None]
+    return out.T, gd[None], gu[None]
 
 
 adapter_gain = 2.0

time: 130 us -> 120 us (0.923)
  Pallas kernels: 122 us -> 112 us
    pallas_call x1, Pallas kernels: 122 us -> 112 us  [fused_device(): pl.pallas_call(functools.partial(fused, n), out_shape=(jax.ShapeDtypeStru...]
where the time goes in v2:
time: 120 us
  Pallas kernels  112 us (93%)
  local copies, waits for them, and re-layouts  6.9 us (6%)
    pallas_call x1, Pallas kernels, fused_device(): pl.pallas_call(functools.partial(fused, n), out_shape=(jax.ShapeDtypeStru...  112 us
    unnamed x6, local copies, waits for them, and re-layouts  6.9 us

profile of v2, /device:TPU:3, one launch (start us, length us, event | category | flops | bytes accessed | tf_op | source)
XLA Modules:
  0.0 119.5 jit_solution(792560288563072693)
XLA Ops:
  0.6 1.4 %copy.13.mid_h = bf16[128,64]{1,0:T(8,128)(2,1)} copy(bf16[128,64]{0,1:T(8,128)(2,1)} %param.12) | data formatting | bytes 32768 | tf_op args[2]
  2.1 112.0 %fused_backward.1 = (bf16[3712,128]{1,0:T(8,128)(2,1)}, f32[64,3712]{1,0:T(8,128)}, f32[64,3968]{1,0:T(8,128)}) custom-call(s32[4,4]{1,0:T(4,128)} %len_s.1, s32[4,4]{1,0:T(4,128)} %doc_s.1, s32[4]{0:T(128)} %row_s.1, bf16[128,3968]{1,0:T(8,128)(2,1)} %g_h.1, bf16[128,3712]{1,0:T(8,128)(2,1)} %x_h.1, bf16[128,64]{1,0:T(8,128)(2,1)} %copy.13.mid_h, ...), custom_call_target="tpu_custom_call" | custom-call | flops 15082717184 | bytes 29458432 | tf_op jit(solution)/shard_map/fused_backward/pallas_call | solution.py:497
  114.0 0.0 copy-start
  114.1 2.3 %copy.14 = bf16[128,3712]{1,0:T(8,128)(2,1)} copy(bf16[128,3712]{0,1:T(8,128)(2,1)} %bitcast.7) | data formatting | bytes 1900544
  116.4 2.2 %copy.17 = f32[1,64,3712]{2,1,0:T(8,128)} copy(f32[1,64,3712]{2,1,0:T(8,128)} %bitcast.6) | data formatting | bytes 1900544
  118.6 0.0 copy-done
  118.6 1.0 copy.18
Async XLA Ops:
  114.0 4.5 %copy-start = (f32[64,3968]{1,0:T(8,128)S(1)}, f32[64,3968]{1,0:T(8,128)}, u32[]{:S(2)}) copy-start(f32[64,3968]{1,0:T(8,128)} %get-tuple-element.8) | copy-start | bytes 3047428
